TPU v7x, 128 devices: a whole 4x4x4 slice. The times are simulated.
128 devices in a mesh: dp: 8 (over z, core), fsdp: 16 (over y, x).
Axes of the slice: x: 4, y: 4, z: 4, core: 2. Of those that a mesh axis runs over, the one named last changes fastest.
Arguments:
- entry_embeddings: bfloat16 [8, 1024, 4, 512], P('dp', 'fsdp'), may hold values from -6 to 6
- norm_scales: bfloat16 [2, 3, 512], P(None, None, ('dp', 'fsdp')), may hold values from 0.5 to 1.5
- triple_entry_matrix: bfloat16 [2, 2, 512, 1536], P(None, None, ('dp', 'fsdp')), may hold values from -0.25 to 0.25
- mixing_exit_matrix: bfloat16 [2, 2, 512, 512], P(None, None, ('dp', 'fsdp')), may hold values from -0.75 to 0.75
- exit_bias: bfloat16 [2, 2, 512], P(None, None, ('dp', 'fsdp')), may hold values from -4 to 4
- expanding_matrix: bfloat16 [2, 512, 2048], P(None, ('dp', 'fsdp')), may hold values from -0.25 to 0.25
- former_dense_bias: bfloat16 [2, 2048], P(None, ('dp', 'fsdp')), may hold values from -6 to 6
- contracting_matrix: bfloat16 [2, 2048, 512], P(None, ('dp', 'fsdp')), may hold values from -0.125 to 0.125
- latter_dense_bias: bfloat16 [2, 512], P(None, ('dp', 'fsdp')), may hold values from -4 to 4
- row_presence_indicator: int32 [8, 1024], P('dp'), may hold values from 0 to 1, as said below
- problem_column_number: int32 [8], P('dp'), may hold values from 1 to 4
- loss_gradient: bfloat16 [8, 1024, 4, 512], P('dp', 'fsdp'), may hold values from -6 to 6
Outputs:
- activations: float32 [8, 1024, 4, 512], P('dp', 'fsdp')
- delta_tokens: float32 [8, 1024, 4, 512], P('dp', 'fsdp')
- delta_gains: float32 [2, 3, 512], P(None, None, ('dp', 'fsdp'))
- delta_heads: float32 [2, 2, 512, 1536], P(None, None, ('dp', 'fsdp'))
- delta_merge: float32 [2, 2, 512, 512], P(None, None, ('dp', 'fsdp'))
- delta_offsets: float32 [2, 2, 512], P(None, None, ('dp', 'fsdp'))
- delta_inner: float32 [2, 512, 2048], P(None, ('dp', 'fsdp'))
- delta_thresholds: float32 [2, 2048], P(None, ('dp', 'fsdp'))
- delta_outer: float32 [2, 2048, 512], P(None, ('dp', 'fsdp'))
- delta_baselines: float32 [2, 512], P(None, ('dp', 'fsdp'))
Inputs may be any that keep to these rules, and one draw needn't show every extreme that they name: `row_presence_indicator`: the first and the last of the 1024 sample slots of every task are real. Feature slots with index problem_column_number or more are padding.
All inputs are finite; a program needn't handle non-finite values.
Results may differ from a plain program's by a relative error of at most 0.033.
Values may be sent and summed in bfloat16 or wider, within the bound.
A program may use at most 192 MiB of HBM per device.

v0:
```python
import math

import jax
import jax.numpy as jnp
from jax import lax
from jax.sharding import PartitionSpec as P

HEADS = 8
BLOCK_TOTAL = 2


EPS = 1e-05
NEG = -1e30
SAMPLE_FORMS = ("ifhc,jfhc->fhij", "fhij,jfhc->ifhc", "fhij,ifhc->jfhc")
FEATURE_FORMS = ("sihc,sjhc->shij", "shij,sjhc->sihc", "shij,sihc->sjhc")


def normalize(rows, gain):
    mean = jnp.mean(rows, axis=-1, keepdims=True)
    centred = rows - mean
    spread = jnp.mean(centred * centred, axis=-1, keepdims=True)
    return centred * lax.rsqrt(spread + EPS) * gain


def smooth(values):
    return jax.nn.gelu(values, approximate=True)


def project(left, right):
    return jnp.einsum("sfd,de->sfe", left, right, preferred_element_type=jnp.float32)


def project_back(left, right):
    return jnp.einsum("sfe,de->sfd", left, right, preferred_element_type=jnp.float32)


def outer_sum(left, right):
    return jnp.einsum("sfd,sfe->de", left, right, preferred_element_type=jnp.float32)


def token_sum(values):
    return jnp.sum(values.astype(jnp.float32), axis=(0, 1))


def split_heads(rows):
    return rows.reshape(rows.shape[:-1] + (HEADS, rows.shape[-1] // HEADS))


def join_heads(rows):
    return rows.reshape(rows.shape[:-2] + (rows.shape[-2] * rows.shape[-1],))


def score_block(query, keys, key_ok, forms):
    scale = 1.0 / math.sqrt(query.shape[-1])
    raw = jnp.einsum(forms[0], query, keys, preferred_element_type=jnp.float32) * scale
    return jnp.where(key_ok, raw, NEG)


def attend_forward(query, keys, values, key_ok, forms):
    scores = score_block(query, keys, key_ok, forms)
    top = jnp.max(scores, axis=-1, keepdims=True)
    expo = jnp.exp(scores - top)
    total = jnp.sum(expo, axis=-1, keepdims=True)
    probs = (expo / total).astype(jnp.bfloat16)
    mixed = jnp.einsum(forms[1], probs, values, preferred_element_type=jnp.float32).astype(
        jnp.bfloat16
    )
    return (join_heads(mixed), top + jnp.log(total))


def attend_backward(query, keys, values, key_ok, logsum, upstream, forms):
    scale = 1.0 / math.sqrt(query.shape[-1])
    scores = score_block(query, keys, key_ok, forms)
    probs = jnp.exp(scores - logsum)
    dprobs = jnp.einsum(forms[0], upstream, values, preferred_element_type=jnp.float32)
    rowsum = jnp.sum(probs * dprobs, axis=-1, keepdims=True)
    dscores = (probs * (dprobs - rowsum)).astype(jnp.bfloat16)
    dquery = jnp.einsum(forms[1], dscores, keys, preferred_element_type=jnp.float32) * scale
    dkeys = jnp.einsum(forms[2], dscores, query, preferred_element_type=jnp.float32) * scale
    dvalues = jnp.einsum(
        forms[2], probs.astype(jnp.bfloat16), upstream, preferred_element_type=jnp.float32
    )
    return (join_heads(dquery), join_heads(dkeys), join_heads(dvalues), rowsum)


def norm_back(rows, gain, upstream):
    pullback = jax.vjp(normalize, rows, gain)[1]
    return pullback(upstream)


def body(
    entry_embeddings,
    norm_scales,
    triple_entry_matrix,
    mixing_exit_matrix,
    exit_bias,
    expanding_matrix,
    former_dense_bias,
    contracting_matrix,
    latter_dense_bias,
    row_presence_indicator,
    problem_column_number,
    loss_gradient,
):
    rows = entry_embeddings.shape[1]
    width = entry_embeddings.shape[3]
    sample_ok = row_presence_indicator[0] > 0
    local_ok = lax.dynamic_slice_in_dim(sample_ok, lax.axis_index("fsdp") * rows, rows)
    feature_ok = jnp.arange(entry_embeddings.shape[2], dtype=jnp.int32) < problem_column_number[0]
    keep = (local_ok[:, None] & feature_ok[None, :])[:, :, None].astype(jnp.float32)
    sample_keys = sample_ok[None, None, None, :]
    feature_keys = feature_ok[None, None, None, :]
    running_representation = entry_embeddings[0].astype(jnp.float32)
    fetched = []
    records = []
    for apply_block in range(BLOCK_TOTAL):
        full = (
            lax.all_gather(norm_scales[apply_block], ("dp", "fsdp"), axis=1, tiled=True),
            lax.all_gather(triple_entry_matrix[apply_block], ("dp", "fsdp"), axis=1, tiled=True),
            lax.all_gather(mixing_exit_matrix[apply_block], ("dp", "fsdp"), axis=1, tiled=True),
            lax.all_gather(exit_bias[apply_block], ("dp", "fsdp"), axis=1, tiled=True),
            lax.all_gather(expanding_matrix[apply_block], ("dp", "fsdp"), axis=0, tiled=True),
            lax.all_gather(former_dense_bias[apply_block], ("dp", "fsdp"), axis=0, tiled=True),
            lax.all_gather(contracting_matrix[apply_block], ("dp", "fsdp"), axis=0, tiled=True),
            lax.all_gather(latter_dense_bias[apply_block], ("dp", "fsdp"), axis=0, tiled=True),
        )
        fetched.append(full)
        (
            gain_full,
            heads_full,
            merge_full,
            offset_full,
            inner_full,
            thresh_full,
            outer_full,
            base_full,
        ) = full
        scales = gain_full.astype(jnp.float32)
        first_in = running_representation
        arows = normalize(running_representation, scales[0]).astype(jnp.bfloat16)
        packed = project(arows, heads_full[0]).astype(jnp.bfloat16)
        keyval = lax.all_gather(packed[..., width:], "fsdp", axis=0, tiled=True)
        mixed, logsum = attend_forward(
            split_heads(packed[..., :width]),
            split_heads(keyval[..., :width]),
            split_heads(keyval[..., width:]),
            sample_keys,
            SAMPLE_FORMS,
        )
        running_representation = (
            running_representation
            + project(mixed, merge_full[0])
            + offset_full[0].astype(jnp.float32)
        )
        second_in = running_representation
        frows = normalize(running_representation, scales[1]).astype(jnp.bfloat16)
        fpacked = project(frows, heads_full[1]).astype(jnp.bfloat16)
        fmixed, flogsum = attend_forward(
            split_heads(fpacked[..., :width]),
            split_heads(fpacked[..., width : 2 * width]),
            split_heads(fpacked[..., 2 * width :]),
            feature_keys,
            FEATURE_FORMS,
        )
        running_representation = (
            running_representation
            + project(fmixed, merge_full[1])
            + offset_full[1].astype(jnp.float32)
        )
        third_in = running_representation
        crows = normalize(running_representation, scales[2]).astype(jnp.bfloat16)
        pre = project(crows, inner_full) + thresh_full.astype(jnp.float32)
        nonlinear_map = smooth(pre).astype(jnp.bfloat16)
        running_representation = (
            running_representation
            + project(nonlinear_map, outer_full)
            + base_full.astype(jnp.float32)
        )
        records.append(
            (
                first_in,
                arows,
                packed,
                keyval,
                logsum,
                mixed,
                second_in,
                frows,
                fpacked,
                flogsum,
                fmixed,
                third_in,
                crows,
                pre,
                nonlinear_map,
            )
        )
    grad = loss_gradient[0].astype(jnp.float32) * keep
    sums = [None] * BLOCK_TOTAL
    for apply_block in reversed(range(BLOCK_TOTAL)):
        full = (
            lax.all_gather(norm_scales[apply_block], ("dp", "fsdp"), axis=1, tiled=True),
            lax.all_gather(triple_entry_matrix[apply_block], ("dp", "fsdp"), axis=1, tiled=True),
            lax.all_gather(mixing_exit_matrix[apply_block], ("dp", "fsdp"), axis=1, tiled=True),
            lax.all_gather(exit_bias[apply_block], ("dp", "fsdp"), axis=1, tiled=True),
            lax.all_gather(expanding_matrix[apply_block], ("dp", "fsdp"), axis=0, tiled=True),
            lax.all_gather(former_dense_bias[apply_block], ("dp", "fsdp"), axis=0, tiled=True),
            lax.all_gather(contracting_matrix[apply_block], ("dp", "fsdp"), axis=0, tiled=True),
            lax.all_gather(latter_dense_bias[apply_block], ("dp", "fsdp"), axis=0, tiled=True),
        )
        (
            gain_full,
            heads_full,
            merge_full,
            offset_full,
            inner_full,
            thresh_full,
            outer_full,
            base_full,
        ) = full
        scales = gain_full.astype(jnp.float32)
        (
            first_in,
            arows,
            packed,
            keyval,
            logsum,
            mixed,
            second_in,
            frows,
            fpacked,
            flogsum,
            fmixed,
            third_in,
            crows,
            pre,
            nonlinear_map,
        ) = records[apply_block]
        down = grad.astype(jnp.bfloat16)
        delta_outer = outer_sum(nonlinear_map, down)
        delta_base = token_sum(down)
        dact = project_back(down, outer_full)
        dpre = jax.vjp(smooth, pre)[1](dact)[0].astype(jnp.bfloat16)
        delta_inner = outer_sum(crows, dpre)
        delta_thresh = token_sum(dpre)
        dstate, gain_three = norm_back(third_in, scales[2], project_back(dpre, inner_full))
        grad = grad + dstate
        down = grad.astype(jnp.bfloat16)
        merge_feature = outer_sum(fmixed, down)
        offset_feature = token_sum(down)
        upstream = split_heads(project_back(down, merge_full[1]).astype(jnp.bfloat16))
        dquery, dkeys, dvalues, unused = attend_backward(
            split_heads(fpacked[..., :width]),
            split_heads(fpacked[..., width : 2 * width]),
            split_heads(fpacked[..., 2 * width :]),
            feature_keys,
            flogsum,
            upstream,
            FEATURE_FORMS,
        )
        dpacked = jnp.concatenate([dquery, dkeys, dvalues], axis=-1).astype(jnp.bfloat16)
        heads_feature = outer_sum(frows, dpacked)
        dstate, gain_two = norm_back(second_in, scales[1], project_back(dpacked, heads_full[1]))
        grad = grad + dstate
        down = grad.astype(jnp.bfloat16)
        merge_sample = outer_sum(mixed, down)
        offset_sample = token_sum(down)
        upstream = split_heads(project_back(down, merge_full[0]).astype(jnp.bfloat16))
        query_local = split_heads(packed[..., :width])
        dquery, dkeys, dvalues, rowsum = attend_backward(
            query_local,
            split_heads(keyval[..., :width]),
            split_heads(keyval[..., width:]),
            sample_keys,
            logsum,
            upstream,
            SAMPLE_FORMS,
        )
        owned = lax.psum_scatter(
            jnp.concatenate([dkeys, dvalues], axis=-1).astype(jnp.bfloat16),
            "fsdp",
            scatter_dimension=0,
            tiled=True,
        ).astype(jnp.float32)
        dpacked = jnp.concatenate([dquery, owned], axis=-1).astype(jnp.bfloat16)
        heads_sample = outer_sum(arows, dpacked)
        dstate, gain_one = norm_back(first_in, scales[0], project_back(dpacked, heads_full[0]))
        grad = grad + dstate
        sums[apply_block] = (
            lax.psum_scatter(
                jnp.stack([gain_one, gain_two, gain_three]),
                ("dp", "fsdp"),
                scatter_dimension=1,
                tiled=True,
            ),
            lax.psum_scatter(
                jnp.stack([heads_sample, heads_feature]),
                ("dp", "fsdp"),
                scatter_dimension=1,
                tiled=True,
            ),
            lax.psum_scatter(
                jnp.stack([merge_sample, merge_feature]),
                ("dp", "fsdp"),
                scatter_dimension=1,
                tiled=True,
            ),
            lax.psum_scatter(
                jnp.stack([offset_sample, offset_feature]),
                ("dp", "fsdp"),
                scatter_dimension=1,
                tiled=True,
            ),
            lax.psum_scatter(delta_inner, ("dp", "fsdp"), scatter_dimension=0, tiled=True),
            lax.psum_scatter(delta_thresh, ("dp", "fsdp"), scatter_dimension=0, tiled=True),
            lax.psum_scatter(delta_outer, ("dp", "fsdp"), scatter_dimension=0, tiled=True),
            lax.psum_scatter(delta_base, ("dp", "fsdp"), scatter_dimension=0, tiled=True),
        )
    stacked = [
        jnp.stack([sums[level][member] for level in range(BLOCK_TOTAL)]) for member in range(8)
    ]
    return (
        (running_representation * keep)[None],
        grad[None],
        stacked[0],
        stacked[1],
        stacked[2],
        stacked[3],
        stacked[4],
        stacked[5],
        stacked[6],
        stacked[7],
    )


def solution(mesh):
    placed = (
        P("dp", "fsdp", None, None),
        P(None, None, ("dp", "fsdp")),
        P(None, None, ("dp", "fsdp"), None),
        P(None, None, ("dp", "fsdp"), None),
        P(None, None, ("dp", "fsdp")),
        P(None, ("dp", "fsdp"), None),
        P(None, ("dp", "fsdp")),
        P(None, ("dp", "fsdp"), None),
        P(None, ("dp", "fsdp")),
        P("dp", None),
        P("dp"),
        P("dp", "fsdp", None, None),
    )
    return jax.shard_map(
        body,
        mesh=mesh,
        in_specs=placed,
        out_specs=(
            P("dp", "fsdp", None, None),
            P("dp", "fsdp", None, None),
            P(None, None, ("dp", "fsdp")),
            P(None, None, ("dp", "fsdp"), None),
            P(None, None, ("dp", "fsdp"), None),
            P(None, None, ("dp", "fsdp")),
            P(None, ("dp", "fsdp"), None),
            P(None, ("dp", "fsdp")),
            P(None, ("dp", "fsdp"), None),
            P(None, ("dp", "fsdp")),
        ),
        check_vma=False,
    )
```

profile of v0, /device:TPU:1, one launch (start us, length us, event | category | flops | bytes accessed | tf_op | source)
XLA Modules:
  0.0 2574.5 jit_solution(11959548542678708248)
XLA Ops:
  11.7 63.3 %all-gather = bf16[1,3,512]{1,0,2:T(2,128)(2,1)S(1)} all-gather(bf16[1,3,4]{1,0,2:T(2,128)(2,1)S(1)} %copy.375), channel_id=2, replica_groups=mesh['dp'=8,'fsdp'=16] {'dp','fsdp'}, dimensions={2}, use_global_device_ids=true | all-gather | bytes 3096 | tf_op jit(solution)/shard_map/all_gather | solution.py:118
  82.5 8.7 fusion.199
  97.8 61.0 %all-gather.3 = bf16[1,2,512]{1,0,2:T(2,128)(2,1)S(1)} all-gather(bf16[1,2,4]{1,0,2:T(2,128)(2,1)S(1)} %copy.380), channel_id=5, replica_groups=mesh['dp'=8,'fsdp'=16] {'dp','fsdp'}, dimensions={2}, use_global_device_ids=true | all-gather | bytes 2064 | tf_op jit(solution)/shard_map/all_gather | solution.py:121
  163.8 65.7 %all-reduce.20 = (bf16[512]{0:T(512)(128)(2,1)S(1)}, bf16[2048]{0:T(1024)(128)(2,1)S(1)}, bf16[512]{0:T(512)(128)(2,1)}, bf16[2048]{0:T(1024)(128)(2,1)}) all-reduce(bf16[512]{0:T(512)(128)(2,1)S(1)} %dynamic-update-slice.1, bf16[2048]{0:T(1024)(128)(2,1)S(1)} %dynamic-update-slice, ...), channel_id=9, replica_groups=mesh['dp'=8,'fsdp'=16] {'dp','fsdp'}, use_global_device_ids=true, to_apply=%add.1 | all-reduce | flops 5120 | bytes 20480
  230.9 58.3 %all-gather.8 = bf16[1,3,512]{1,0,2:T(2,128)(2,1)S(1)} all-gather(bf16[1,3,4]{1,0,2:T(2,128)(2,1)S(1)} %copy.384), channel_id=10, replica_groups=mesh['dp'=8,'fsdp'=16] {'dp','fsdp'}, dimensions={2}, use_global_device_ids=true | all-gather | bytes 3096 | tf_op jit(solution)/shard_map/all_gather | solution.py:118
  299.1 9.4 fusion.198
  314.4 6.4 copy.279
  320.8 6.4 copy.278
  336.1 14.7 fusion.55
  369.7 50.7 %all-gather.37.cloned.1.call-done = bf16[1,2048,512]{2,1,0:T(8,128)(2,1)} async-done(((bf16[1,16,512]{2,1,0:T(8,128)(2,1)}), bf16[1,2048,512]{2,1,0:T(8,128)(2,1)}) %all-gather.37.cloned.1.call-update) | async-done | bytes 2097168 | tf_op jit(solution)/shard_map/all_gather | solution.py:124
  427.1 57.0 %all-gather.11 = bf16[1,2,512]{1,0,2:T(2,128)(2,1)S(1)} all-gather(bf16[1,2,4]{1,0,2:T(2,128)(2,1)S(1)} %copy.389), channel_id=13, replica_groups=mesh['dp'=8,'fsdp'=16] {'dp','fsdp'}, dimensions={2}, use_global_device_ids=true | all-gather | bytes 2064 | tf_op jit(solution)/shard_map/all_gather | solution.py:121
  494.0 60.7 %all-gather.29.cloned.1.call-done = bf16[1024,4,1024]{2,0,1:T(8,128)(2,1)} async-done(((bf16[64,4,1024]{2,0,1:T(8,128)(2,1)}), bf16[1024,4,1024]{2,0,1:T(8,128)(2,1)}) %all-gather.29.cloned.1.call-update) | async-done | bytes 8388624 | tf_op jit(solution)/shard_map/all_gather | solution.py:142
  560.4 6.3 copy.298
  566.7 6.3 copy.297
  599.9 25.5 all-gather.43.cloned.1.call-done
  630.5 61.1 %all-gather.45.cloned.1.call-done = bf16[1,2048,512]{2,1,0:T(8,128)(2,1)} async-done(((bf16[1,16,512]{2,1,0:T(8,128)(2,1)}), bf16[1,2048,512]{2,1,0:T(8,128)(2,1)}) %all-gather.45.cloned.1.call-update) | async-done | bytes 2097168 | tf_op jit(solution)/shard_map/all_gather | solution.py:124
  735.1 8.0 multiply_reduce_fusion.1
  743.1 7.9 fusion.14
  756.6 6.2 copy.330
  762.8 6.2 copy.331
  769.0 7.9 pad_maximum_fusion
  785.8 71.9 %reduce-scatter.13.cloned.1.call-done = bf16[64,4,1024]{2,0,1:T(8,128)(2,1)} async-done(((bf16[1024,4,1024]{2,0,1:T(8,128)(2,1)}), bf16[64,4,1024]{2,0,1:T(8,128)(2,1)}) %reduce-scatter.13.cloned.1.call-update) | async-done | bytes 524304 | tf_op jit(solution)/shard_map/reduce_scatter | solution.py:279
  911.8 8.2 multiply_reduce_fusion
  920.0 8.0 fusion.17
  933.6 6.2 copy.349
  939.8 6.2 copy.350
  946.1 7.9 pad_maximum_fusion.1
  990.2 48.4 %reduce-scatter.15.cloned.1.call-done = bf16[64,4,1024]{2,0,1:T(8,128)(2,1)} async-done(((bf16[1024,4,1024]{2,0,1:T(8,128)(2,1)}), bf16[64,4,1024]{2,0,1:T(8,128)(2,1)}) %reduce-scatter.15.cloned.1.call-update) | async-done | bytes 524304 | tf_op jit(solution)/shard_map/reduce_scatter | solution.py:279
  1049.0 606.0 %reduce-scatter.19.cloned.1.call-done = f32[16,512]{1,0:T(8,128)} async-done(((f32[2048,512]{1,0:T(8,128)}), f32[16,512]{1,0:T(8,128)}) %reduce-scatter.19.cloned.1.call-update) | async-done | bytes 32784 | tf_op jit(solution)/shard_map/reduce_scatter | solution.py:316
  1655.1 640.5 %reduce-scatter.17.cloned.1.call-done = f32[16,512]{1,0:T(8,128)} async-done(((f32[2048,512]{1,0:T(8,128)}), f32[16,512]{1,0:T(8,128)}) %reduce-scatter.17.cloned.1.call-update) | async-done | bytes 32784 | tf_op jit(solution)/shard_map/reduce_scatter | solution.py:316
  2300.0 95.3 %all-reduce.18 = (f32[3,512]{1,0:T(4,128)S(1)}, f32[3,512]{1,0:T(4,128)S(1)}, f32[2,512]{1,0:T(2,128)S(1)}, f32[2,512]{1,0:T(2,128)S(1)}, f32[2048]{0:T(1024)S(1...) all-reduce(f32[3,512]{1,0:T(4,128)S(1)} %pad_maximum_fusion.17, ...), channel_id=21, replica_groups=mesh['dp'=8,'fsdp'=16] {'dp','fsdp'}, use_global_device_ids=true, to_apply=%region_45.46.clone | all-reduce | flops 10240 | bytes 81920
  2399.4 163.6 %all-reduce.23.cloned.1.call-done = (f32[2,512,1536]{2,1,0:T(8,128)}, f32[2,512,1536]{2,1,0:T(8,128)}, f32[2,512,512]{2,1,0:T(8,128)}, f32[2,512,512]{2,1,0:T(8,...) async-done(((f32[2,512,1536]{2,1,0:T(8,128)}, f32[2,512,1536]{2,1,0:T(8,128)}, f32[2,512,512]{2,1,0:T(8,128)}, f32[2,512,512]{2,1,0:T(8,128)}, f32[512,2048]{1,0:T(8,128)}, ...) | async-done | bytes 25165840
  (596 shorter events, 297.3 us)
Async XLA Ops:
  7.2 75.3 %all-gather.31.cloned.1.call-start = ((), (), s32[]{:S(2)}) async-start(), calls=%async_computation.10 | async-start | bytes 3170304 | tf_op jit(solution)/shard_map/all_gather | solution.py:119
  8.7 286.1 %all-gather.33.cloned.1.call-start = ((), (), s32[]{:S(2)}) async-start(), calls=%async_computation.11 | async-start | bytes 1056768 | tf_op jit(solution)/shard_map/all_gather | solution.py:120
  10.1 289.0 %all-gather.39.cloned.1.call-start = ((), (), s32[]{:S(2)}) async-start(), calls=%async_computation.14 | async-start | bytes 3170304 | tf_op jit(solution)/shard_map/all_gather | solution.py:119
  10.8 297.7 %all-gather.27.cloned.1.call-start = ((), (), s32[]{:S(2)}) async-start(), calls=%async_computation.4 | async-start | bytes 8912896 | tf_op jit(solution)/shard_map/all_gather | solution.py:142
  82.4 269.1 %copy-start.117 = (f32[512]{0:T(512)}, f32[512]{0:T(512)S(1)}, u32[]{:S(2)}) copy-start(f32[512]{0:T(512)S(1)} %get-tuple-element.78) | copy-start | bytes 6148
  82.4 282.2 %copy-start.71 = (f32[512]{0:T(512)}, f32[512]{0:T(512)S(1)}, u32[]{:S(2)}) copy-start(f32[512]{0:T(512)S(1)} %get-tuple-element.77) | copy-start | bytes 6148
  94.3 270.3 %all-gather.35.cloned.1.call-start = ((), (), s32[]{:S(2)}) async-start(), calls=%async_computation.12 | async-start | bytes 4227072 | tf_op jit(solution)/shard_map/all_gather | solution.py:122
  95.1 325.4 %all-gather.37.cloned.1.call-start = ((), (), s32[]{:S(2)}) async-start(), calls=%async_computation.13 | async-start | bytes 2113536 | tf_op jit(solution)/shard_map/all_gather | solution.py:124
  95.8 393.6 %all-gather.41.cloned.1.call-start = ((), (), s32[]{:S(2)}) async-start(), calls=%async_computation.15 | async-start | bytes 1056768 | tf_op jit(solution)/shard_map/all_gather | solution.py:120
  96.5 458.1 %all-gather.29.cloned.1.call-start = ((), (), s32[]{:S(2)}) async-start(), calls=%async_computation.5 | async-start | bytes 8912896 | tf_op jit(solution)/shard_map/all_gather | solution.py:142
  97.2 653.8 %copy-start.52 = (pred[1024]{0:T(1024)(128)(4,1)}, pred[1024]{0:T(1024)(128)(4,1)S(1)}, u32[]{:S(2)}) copy-start(pred[1024]{0:T(1024)(128)(4,1)S(1)} %get-tuple-element.148) | copy-start | bytes 3076
  162.8 543.8 %copy-start.65 = (pred[4]{0:T(512)(128)(4,1)}, pred[4]{0:T(512)(128)(4,1)S(1)}, u32[]{:S(2)}) copy-start(pred[4]{0:T(512)(128)(4,1)S(1)} %iota_compare_fusion) | copy-start | bytes 16
  294.8 403.6 %copy-start.85 = (f32[512]{0:T(512)}, f32[512]{0:T(512)S(1)}, u32[]{:S(2)}) copy-start(f32[512]{0:T(512)S(1)} %get-tuple-element.72) | copy-start | bytes 6148
  423.8 161.5 %copy-start.15 = (f32[64,4,512]{2,0,1:T(8,128)}, f32[64,4,512]{2,0,1:T(8,128)S(1)}, u32[]{:S(2)}) copy-start(f32[64,4,512]{2,0,1:T(8,128)S(1)} %get-tuple-element.164) | copy-start | bytes 1572868
  425.6 199.8 %all-gather.43.cloned.1.call-start = ((), (), s32[]{:S(2)}) async-start(), calls=%async_computation.16 | async-start | bytes 4227072 | tf_op jit(solution)/shard_map/all_gather | solution.py:122
  426.3 265.2 %all-gather.45.cloned.1.call-start = ((), (), s32[]{:S(2)}) async-start(), calls=%async_computation.17 | async-start | bytes 2113536 | tf_op jit(solution)/shard_map/all_gather | solution.py:124
  426.9 430.8 %reduce-scatter.13.cloned.1.call-start = ((), (), s32[]{:S(2)}) async-start(), calls=%async_computation.6 | async-start | bytes 8912896 | tf_op jit(solution)/shard_map/reduce_scatter | solution.py:279
  585.7 146.2 %copy-start.79 = (f32[64,4]{0,1:T(4,128)}, f32[64,4]{0,1:T(4,128)S(1)}, u32[]{:S(2)}) copy-start(f32[64,4]{0,1:T(4,128)S(1)} %broadcast_multiply_fusion.1) | copy-start | bytes 3076
  599.6 98.8 %copy-start.69 = (f32[64,4]{0,1:T(4,128)}, f32[64,4]{0,1:T(4,128)S(1)}, u32[]{:S(2)}) copy-start(f32[64,4]{0,1:T(4,128)S(1)} %broadcast_multiply_fusion) | copy-start | bytes 3076
  599.8 98.6 %copy-start.87 = (f32[64,4]{0,1:T(4,128)}, f32[64,4]{0,1:T(4,128)S(1)}, u32[]{:S(2)}) copy-start(f32[64,4]{0,1:T(4,128)S(1)} %fusion.168) | copy-start | bytes 3076
  776.9 261.7 %reduce-scatter.15.cloned.1.call-start = ((), (), s32[]{:S(2)}) async-start(), calls=%async_computation.7 | async-start | bytes 8912896 | tf_op jit(solution)/shard_map/reduce_scatter | solution.py:279
  954.0 701.1 %reduce-scatter.19.cloned.1.call-start = ((), (), s32[]{:S(2)}) async-start(), calls=%async_computation.9 | async-start | bytes 4227072 | tf_op jit(solution)/shard_map/reduce_scatter | solution.py:316
  959.3 1336.3 %reduce-scatter.17.cloned.1.call-start = ((), (), s32[]{:S(2)}) async-start(), calls=%async_computation.8 | async-start | bytes 4227072 | tf_op jit(solution)/shard_map/reduce_scatter | solution.py:316
  964.1 1598.9 %all-reduce.23.cloned.1.call-start = ((), (), s32[]{:S(2)}) async-start(), calls=%async_computation.18 | async-start | bytes 50331648
  1044.6 1252.4 %copy-start.151 = (bf16[64,4,1024]{2,0,1:T(8,128)(2,1)S(1)}, bf16[64,4,1024]{2,0,1:T(8,128)(2,1)}, u32[]{:S(2)}) copy-start(bf16[64,4,1024]{2,0,1:T(8,128)(2,1)} %reduce-scatter.15.cloned.1.call-done) | copy-start | bytes 1572868
  1047.7 1251.9 %copy-start.108 = (f32[64,4]{0,1:T(4,128)S(1)}, f32[64,4]{0,1:T(4,128)}, u32[]{:S(2)}) copy-start(f32[64,4]{0,1:T(4,128)} %copy-done.107) | copy-start | bytes 3076
  1047.7 1252.2 %copy-start.127 = (f32[512]{0:T(512)S(1)}, f32[512]{0:T(512)}, u32[]{:S(2)}) copy-start(f32[512]{0:T(512)} %get-tuple-element.60) | copy-start | bytes 6148
  1047.7 1252.2 %copy-start.124 = (f32[512]{0:T(512)S(1)}, f32[512]{0:T(512)}, u32[]{:S(2)}) copy-start(f32[512]{0:T(512)} %get-tuple-element.134) | copy-start | bytes 6148
  1047.8 1252.2 %copy-start.126 = (f32[512]{0:T(512)S(1)}, f32[512]{0:T(512)}, u32[]{:S(2)}) copy-start(f32[512]{0:T(512)} %get-tuple-element.100) | copy-start | bytes 6148
  1047.8 1252.2 %copy-start.135 = (f32[2048]{0:T(1024)S(1)}, f32[2048]{0:T(1024)}, u32[]{:S(2)}) copy-start(f32[2048]{0:T(1024)} %get-tuple-element.184) | copy-start | bytes 24580
  1047.8 1252.2 %copy-start.136 = (f32[2048]{0:T(1024)S(1)}, f32[2048]{0:T(1024)}, u32[]{:S(2)}) copy-start(f32[2048]{0:T(1024)} %get-tuple-element.186) | copy-start | bytes 24580
  1047.8 1348.3 %copy-start.19 = (f32[64,4,512]{2,0,1:T(8,128)S(1)}, f32[64,4,512]{2,0,1:T(8,128)}, u32[]{:S(2)}) copy-start(f32[64,4,512]{2,0,1:T(8,128)} %copy-done.18) | copy-start | bytes 1572868
  (143 other events, 2342.9 us)
Sparse Core Ops, SparseCore 0:
  11.6 69.4 all-gather.30
  84.4 60.9 all-gather.32
  149.0 63.3 all-gather.38
  215.0 68.4 all-gather.26
  287.0 67.1 all-gather.34
  357.7 62.7 all-gather.36
  423.2 61.0 all-gather.40
  487.0 67.5 all-gather.28
  558.4 66.9 all-gather.42
  628.8 62.7 all-gather.44
  777.1 80.5 reduce-scatter.12
  954.1 84.5 reduce-scatter.14
  1041.0 613.9 reduce-scatter.18
  1657.4 638.1 reduce-scatter.16
  2301.9 261.0 all-reduce.22
where the time goes:
time: 2590 us; the launch traced here: 2570 us
  waiting for transfers between devices  1730 us (67%)
  blocking collectives  401 us (15%)
  local copies, waits for them, and re-layouts  188 us (7%)
  matrix products  176 us (7%)
  other arithmetic  63 us (2%)
    reduce_scatter x2, waiting for transfers between devices, body(): lax.psum_scatter(delta_outer, ('dp', 'fsdp'), scatter_dimension=0, tiled=...  1250 us
    unnamed x16, waiting for transfers between devices  164 us
    unnamed x2, blocking collectives  161 us
    all_gather x2, blocking collectives, body(): lax.all_gather(norm_scales[apply_block], ('dp', 'fsdp'), axis=1, tiled=True)  122 us
    reduce_scatter x2, waiting for transfers between devices, body(): lax.psum_scatter(jnp.concatenate([dkeys, dvalues], axis=-1).astype(jnp.bf...  120 us
    all_gather x2, blocking collectives, body(): lax.all_gather(exit_bias[apply_block], ('dp', 'fsdp'), axis=1, tiled=True)  118 us
    all_gather x2, waiting for transfers between devices, body(): lax.all_gather(contracting_matrix[apply_block], ('dp', 'fsdp'), axis=0, t...  112 us
    all_gather x2, waiting for transfers between devices, body(): keyval = lax.all_gather(packed[..., width:], 'fsdp', axis=0, tiled=True)  60.7 us
  transfers between devices with their start and end apart: 15, of which 9 were waited for; matrix products, arithmetic and copies ran while one was open for 9% of the time, Pallas kernels for 0%

commit v1 on v0

v1 whole, which is shorter than its diff:
```python
import functools

import jax
import jax.numpy as jnp
from jax import lax
from jax.experimental import pallas as pl
from jax.experimental.pallas import tpu as pltpu
from jax.sharding import PartitionSpec as P

EPS = 1e-05
NEG = -1e30
F32 = jnp.float32
BF16 = jnp.bfloat16
MESH = pl.DeviceIdType.MESH
LAYERS = 2
TOK = 256
DIM = 512
VECS = 10
SCALE = 0.125

QKV = (0, 512)
OUT = (384, 896)
INNER = 1024
OUTER = 1536

AG_ORDERS = ("xyz", "yzx", "zxy")
AG_GROUPS = (
    (0, ((0, 128), (128, 256), (256, 384))),
    (0, ((384, 1024), (1024, 1536), (1536, 2048))),
    (1, ((0, 640), (640, 1280), (1280, 2048))),
)
RS_ORDERS = ("zyx", "xzy", "yxz")
RS_GROUPS = (
    ((1024, 1280), (1280, 1664), (1664, 2048)),
    ((512, 768), (768, 896), (896, 1024)),
    ((0, 128), (128, 384), (384, 512)),
)


def dot(a, b):
    return jnp.dot(a, b, preferred_element_type=F32)


def dot_nt(a, b):
    return lax.dot_general(a, b, (((1,), (1,)), ((), ())), preferred_element_type=F32)


def turned(a):
    return a.astype(F32).T.astype(BF16)


def colsum(a):
    return jnp.sum(a, axis=0, keepdims=True)


def lane(shape):
    return lax.broadcasted_iota(jnp.int32, shape, len(shape) - 1)


def kernel(
    x_ref,
    seed_ref,
    blocks_ref,
    outer_ref,
    vec_ref,
    kmask_ref,
    fmask_ref,
    hout_ref,
    gout_ref,
    wout_ref,
    w2out_ref,
    vecout_ref,
    G,
    dG,
    recvC,
    R1,
    R2,
    R3,
    fin,
    xin,
    xout,
    xfin,
    vsum,
    vrecv,
    VB,
    gsum,
    grecv,
    H,
    PK,
    QK,
    PKF,
    MX,
    MXF,
    LSE,
    LSEF,
    osend,
    upsend,
    uprecv,
    dsend,
    drecv,
    kh,
    vh,
    tr,
    DK,
    DV,
    abuf,
    dnbuf,
    dacc,
    g_ref,
    a2a_s,
    a2a_r,
    ag_s,
    ag_r,
    agc_s,
    agc_r,
    rs_s,
    rs_r,
    rsc_s,
    rsc_r,
    xs_s,
    xs_r,
    v_s,
    v_r,
    gv_s,
    gv_r,
):
    dp = lax.axis_index("dp")
    fs = lax.axis_index("fsdp")
    me = {"z": lax.div(dp, 2), "c": lax.rem(dp, 2), "y": lax.div(fs, 4), "x": lax.rem(fs, 4)}

    def device(at):
        return (at["z"] * 2 + at["c"], at["y"] * 4 + at["x"])

    def beside(axis, step):
        at = dict(me)
        at[axis] = lax.rem(me[axis] + step, 2 if axis == "c" else 4)
        return at

    def remote(src, dst, send, recv, at):
        return pltpu.make_async_remote_copy(
            src_ref=src,
            dst_ref=dst,
            send_sem=send,
            recv_sem=recv,
            device_id=device(at),
            device_id_type=MESH,
        )

    barrier = pltpu.get_barrier_semaphore()

    def greet(k, carry):
        at = dict(me)
        at["y"] = lax.rem(me["y"] + lax.div(k, 4), 4)
        at["x"] = lax.rem(me["x"] + lax.rem(k, 4), 4)
        pl.semaphore_signal(barrier, inc=1, device_id=device(at), device_id_type=MESH)
        return carry

    lax.fori_loop(1, 16, greet, 0)
    for step in (1, 2, 3):
        pl.semaphore_signal(barrier, inc=1, device_id=device(beside("z", step)), device_id_type=MESH)
    pl.semaphore_signal(barrier, inc=1, device_id=device(beside("c", 1)), device_id_type=MESH)
    pl.semaphore_wait(barrier, 19)

    def x_copies():
        return [
            remote(
                blocks_ref.at[beside("x", d)["x"]],
                xin.at[me["x"]],
                xs_s.at[0, d - 1],
                xs_r.at[0, d - 1],
                beside("x", d),
            )
            for d in (1, 2, 3)
        ]

    def vec_copies(axis, buf, recv, ss, rs, slot):
        return [
            remote(buf, recv.at[slot, d - 1], ss.at[slot, d - 1], rs.at[slot, d - 1], beside(axis, d))
            for d in ((1,) if axis == "c" else (1, 2, 3))
        ]

    def held(ref, at, cols):
        return ref.at[at["z"], at["c"], at["y"], at["x"], :, pl.ds(cols[0], cols[1] - cols[0])]

    ALL = slice(None)

    def ag_copies(group, phase):
        layer, streams = AG_GROUPS[group]
        Gl = G.at[layer]
        if phase == 3:
            part = held(
                Gl, dict(z=ALL, c=me["c"], y=ALL, x=ALL), (streams[0][0], streams[2][1])
            )
            return [remote(part, part, agc_s.at[group], agc_r.at[group], beside("c", 1))]
        out = []
        for s, cols in enumerate(streams):
            order = AG_ORDERS[s]
            at = dict(me)
            for axis in order[:phase]:
                at[axis] = ALL
            part = held(Gl, at, cols)
            for d in (1, 2, 3):
                n = phase * 3 + d - 1
                out.append(
                    remote(
                        part,
                        part,
                        ag_s.at[group, s, n],
                        ag_r.at[group, s, n],
                        beside(order[phase], d),
                    )
                )
        return out

    def start(copies):
        for copy in copies:
            copy.start()

    def arrive(copies):
        for copy in copies:
            copy.wait_recv()

    def leave(copies):
        for copy in copies:
            copy.wait_send()

    def ag_step(group, phase):
        if phase > 0:
            arrive(ag_copies(group, phase - 1))
        if phase < 4:
            start(ag_copies(group, phase))

    def a2a_each(n, src, dst, act):
        def one(k, carry):
            at = dict(me)
            at["y"] = lax.rem(me["y"] + lax.div(k, 4), 4)
            at["x"] = lax.rem(me["x"] + lax.rem(k, 4), 4)
            act(remote(src(at["y"], at["x"]), dst, a2a_s.at[n, k], a2a_r.at[n, k], at))
            return carry

        lax.fori_loop(1, 16, one, 0)

    def a2a_start(n, src, dst):
        a2a_each(n, src, dst, lambda c: c.start())
        dst[...] = src(me["y"], me["x"])[...]

    def a2a_wait(n, src, dst):
        a2a_each(n, src, dst, lambda c: c.wait())

    def vector(layer, j):
        return VB[layer * VECS + j]

    def ln_parts(v):
        mean = jnp.mean(v, axis=-1, keepdims=True)
        cen = v - mean
        r = lax.rsqrt(jnp.mean(cen * cen, axis=-1, keepdims=True) + EPS)
        return cen * r, r

    def ln_forward(layer, k):
        gain = vector(layer, k)

        def rows(i, carry):
            at = pl.ds(pl.multiple_of(i * 64, 64), 64)
            hat, unused = ln_parts(H[layer, k, at, :])
            abuf[at, :] = (hat * gain).astype(BF16)
            return carry

        lax.fori_loop(0, 4, rows, 0)

    def ln_backward(layer, k):
        gain = vector(layer, k)

        def rows(i, total):
            at = pl.ds(pl.multiple_of(i * 64, 64), 64)
            hat, r = ln_parts(H[layer, k, at, :])
            dy = dacc[at, :]
            t = dy * gain
            back = r * (
                t
                - jnp.mean(t, axis=-1, keepdims=True)
                - hat * jnp.mean(t * hat, axis=-1, keepdims=True)
            )
            g_ref[at, :] = g_ref[at, :] + back
            return total + colsum(dy * hat)

        put_vector(layer, k, lax.fori_loop(0, 4, rows, jnp.zeros((1, DIM), F32)))

    def put_vector(layer, j, row):
        for t in range(4):
            at = (layer * VECS + j) * 4 + t
            gsum[at : at + 1, :] = row[:, t * 128 : (t + 1) * 128]

    def weight_cols(layer, g, first, width):
        return G[layer, :, :, :, g, :, first : first + width].reshape(DIM, width)

    def out_matrix(layer, k):
        return jnp.concatenate([weight_cols(layer, g, OUT[k], 128) for g in range(4)], axis=1)

    def project(layer, k, dst):
        def cols(g, carry):
            dst[:, g] = (
                dot(abuf[...], weight_cols(layer, g, QKV[k], 384)).astype(BF16).reshape(4, 64, 384)
            )
            return carry

        lax.fori_loop(0, 4, cols, 0)

    def join(mx):
        return jnp.concatenate([mx[:, p].reshape(TOK, 128) for p in range(4)], axis=1)

    def attention_out(layer, k, mx):
        H[layer, k + 1] = (
            H[layer, k] + dot(join(mx), out_matrix(layer, k)) + vector(layer, 3 + k)
        )

    def head_lanes(shape, h):
        where = lane(shape)
        return (where >= h * 64) & (where < (h + 1) * 64)

    def sample_prepare(layer, backward):
        k = QK[layer, :, :, 128:256].reshape(1024, 128)
        v = QK[layer, :, :, 256:384].reshape(1024, 128)
        where = lane((1024, 128))
        zero = jnp.zeros((1024, 128), BF16)
        for h in range(2):
            mine = head_lanes((1024, 128), h)
            kh[h] = jnp.where(mine, k, jnp.where(where == 64 * (1 - h), kmask_ref[...], zero))
            if backward:
                vh[h] = jnp.where(mine, v, zero)
        tr[...] = turned(k if backward else v)

    def sample_query(layer, i):
        return QK[layer, pl.ds(i * 4, 4), :, 0:128].reshape(256, 128) * jnp.asarray(SCALE, BF16)

    def with_one(q, h):
        return jnp.where(lane((256, 128)) == 64 * (1 - h), jnp.ones((256, 128), BF16), q)

    def sample_forward(layer):
        sample_prepare(layer, False)

        def block(i, carry):
            q = sample_query(layer, i)
            parts = []
            for h in range(2):
                s = dot_nt(kh[h], with_one(q, h))
                top = jnp.max(s, axis=0, keepdims=True)
                e = jnp.exp(s - top)
                total = colsum(e)
                LSE[layer, h, i] = top + jnp.log(total)
                parts.append(dot(tr[h * 64 : (h + 1) * 64, :], e.astype(BF16)) / total)
            mixed = jnp.concatenate(parts, axis=0).T.astype(BF16)
            osend[pl.ds(i * 4, 4)] = mixed.reshape(4, 64, 128)
            return carry

        lax.fori_loop(0, 4, block, 0)

    def sample_backward(layer):
        sample_prepare(layer, True)

        def block(i, carry):
            q = sample_query(layer, i)
            up = uprecv[layer, pl.ds(i * 4, 4)].reshape(256, 128)
            parts = []
            for h in range(2):
                s = dot_nt(kh[h], with_one(q, h))
                p = jnp.exp(s - LSE[layer, h, i])
                dprobs = dot_nt(vh[h], up)
                t = p * dprobs
                ds = (t - p * colsum(t)).astype(BF16)
                dv = dot(p.astype(BF16), up)
                dk = dot(ds, q)

                @pl.when(i == 0)
                def _():
                    DV[h] = dv
                    DK[h] = dk

                @pl.when(i > 0)
                def _():
                    DV[h] = DV[h] + dv
                    DK[h] = DK[h] + dk

                parts.append(dot(tr[h * 64 : (h + 1) * 64, :], ds))
            dq = (jnp.concatenate(parts, axis=0).T * SCALE).astype(BF16)
            dsend[pl.ds(i * 4, 4), :, 0:128] = dq.reshape(4, 64, 128)
            return carry

        lax.fori_loop(0, 4, block, 0)
        first = head_lanes((1024, 128), 0)
        dsend[:, :, 128:256] = jnp.where(first, DK[0], DK[1]).astype(BF16).reshape(16, 64, 128)
        dsend[:, :, 256:384] = jnp.where(first, DV[0], DV[1]).astype(BF16).reshape(16, 64, 128)

    def feature_parts(layer, p):
        q = PKF[layer, :, p, :, 0:128].reshape(TOK, 128) * jnp.asarray(SCALE, BF16)
        k = PKF[layer, :, p, :, 128:256].reshape(TOK, 128)
        v = PKF[layer, :, p, :, 256:384].reshape(TOK, 128)
        return q, k, v

    def feature_forward(layer):
        zero = jnp.zeros((TOK, 128), BF16)

        def pair(p, carry):
            q, k, v = feature_parts(layer, p)
            vt = turned(v)
            parts = []
            for h in range(2):
                mine = head_lanes((TOK, 128), h)
                s = dot_nt(jnp.where(mine, k, zero), q) + fmask_ref[...]
                top = jnp.max(s, axis=0, keepdims=True)
                e = jnp.exp(s - top)
                total = colsum(e)
                LSEF[layer, h, p] = top + jnp.log(total)
                parts.append(dot(vt[h * 64 : (h + 1) * 64, :], e.astype(BF16)) / total)
            MXF[layer, :, p] = jnp.concatenate(parts, axis=0).T.astype(BF16).reshape(4, 64, 128)
            return carry

        lax.fori_loop(0, 4, pair, 0)

    def feature_backward(layer):
        zero = jnp.zeros((TOK, 128), BF16)

        def pair(p, carry):
            q, k, v = feature_parts(layer, p)
            up = upsend[:, p].reshape(TOK, 128)
            kt = turned(k)
            dqs, dks, dvs = [], [], []
            for h in range(2):
                mine = head_lanes((TOK, 128), h)
                s = dot_nt(jnp.where(mine, k, zero), q) + fmask_ref[...]
                probs = jnp.exp(s - LSEF[layer, h, p])
                dprobs = dot_nt(jnp.where(mine, v, zero), up)
                t = probs * dprobs
                ds = (t - probs * colsum(t)).astype(BF16)
                dvs.append(dot(probs.astype(BF16), up))
                dks.append(dot(ds, q))
                dqs.append(dot(kt[h * 64 : (h + 1) * 64, :], ds))
            first = head_lanes((TOK, 128), 0)
            dq = (jnp.concatenate(dqs, axis=0).T * SCALE).astype(BF16)
            drecv[:, p, :, 0:128] = dq.reshape(4, 64, 128)
            dk = jnp.where(first, dks[0], dks[1]).astype(BF16)
            drecv[:, p, :, 128:256] = dk.reshape(4, 64, 128)
            dv = jnp.where(first, dvs[0], dvs[1]).astype(BF16)
            drecv[:, p, :, 256:384] = dv.reshape(4, 64, 128)
            return carry

        lax.fori_loop(0, 4, pair, 0)

    def outer_block(layer, g):
        return G[layer, g, :, :, :, :, OUTER : OUTER + 512].reshape(DIM, DIM)

    def gelu_parts(pre):
        inner = 0.7978845608028654 * (pre + 0.044715 * (pre * pre * pre))
        th = jnp.tanh(inner)
        return th

    def ff_forward(layer, last):
        ln_forward(layer, 2)
        dacc[...] = H[layer, 2] + vector(layer, 5)

        def cols(g, carry):
            pre = dot(abuf[...], weight_cols(layer, g, INNER, 512)) + VB[layer * VECS + 6 + g]
            act = (0.5 * pre * (1.0 + gelu_parts(pre))).astype(BF16)
            dacc[...] = dacc[...] + dot(act, outer_block(layer, g))
            return carry

        lax.fori_loop(0, 4, cols, 0)
        if last:
            hout_ref[...] = dacc[...]
        else:
            H[layer + 1, 0] = dacc[...]

    def round_gradient(layer, j):
        down = g_ref[...].astype(BF16)
        dnbuf[...] = down
        put_vector(layer, j, colsum(down.astype(F32)))

    def ff_backward(layer):
        round_gradient(layer, 5)
        ln_forward(layer, 2)

        def cols(g, carry):
            w1 = weight_cols(layer, g, INNER, 512)
            pre = dot(abuf[...], w1) + VB[layer * VECS + 6 + g]
            th = gelu_parts(pre)
            half = 0.5 * (1.0 + th)
            act = (pre * half).astype(BF16)
            slope = half + 0.5 * pre * (1.0 - th * th) * (
                0.7978845608028654 * (1.0 + 3 * 0.044715 * (pre * pre))
            )
            dact = dot_nt(dnbuf[...], outer_block(layer, g))
            dpre = (dact * slope).astype(BF16)
            dG[layer, g, :, :, :, :, OUTER : OUTER + 512] = (
                dot(turned(act), dnbuf[...]).astype(BF16).reshape(2, 4, 4, 16, 512)
            )
            dG[layer, :, :, :, g, :, INNER : INNER + 512] = (
                dot(turned(abuf[...]), dpre).astype(BF16).reshape(4, 2, 4, 16, 512)
            )
            dc = dot_nt(dpre, w1)

            @pl.when(g == 0)
            def _():
                dacc[...] = dc

            @pl.when(g > 0)
            def _():
                dacc[...] = dacc[...] + dc

            row = colsum(dpre.astype(F32))
            for t in range(4):
                gsum[pl.ds((layer * VECS + 6 + g) * 4 + t, 1), :] = row[:, t * 128 : (t + 1) * 128]
            return carry

        lax.fori_loop(0, 4, cols, 0)
        ln_backward(layer, 2)

    def attention_out_backward(layer, k, mx):
        round_gradient(layer, 3 + k)
        down = dnbuf[...]
        dwo = dot(turned(join(mx)), down).astype(BF16)
        for g in range(4):
            dG[layer, :, :, :, g, :, OUT[k] : OUT[k] + 128] = dwo[:, g * 128 : (g + 1) * 128].reshape(
                4, 2, 4, 16, 128
            )
        up = dot_nt(down, out_matrix(layer, k)).astype(BF16)
        for p in range(4):
            upsend[:, p] = up[:, p * 128 : (p + 1) * 128].reshape(4, 64, 128)

    def project_backward(layer, k):
        ln_forward(layer, k)
        at = turned(abuf[...])

        def cols(g, carry):
            d = drecv[:, g].reshape(TOK, 384)
            w = weight_cols(layer, g, QKV[k], 384)
            dG[layer, :, :, :, g, :, QKV[k] : QKV[k] + 384] = (
                dot(at, d).astype(BF16).reshape(4, 2, 4, 16, 384)
            )
            da = dot_nt(d, w)

            @pl.when(g == 0)
            def _():
                dacc[...] = da

            @pl.when(g > 0)
            def _():
                dacc[...] = dacc[...] + da

            return carry

        lax.fori_loop(0, 4, cols, 0)
        ln_backward(layer, k)

    def rest(order, phase):
        return "".join(a for a in "zyx" if a not in order[:phase])

    def rs_copies(layer, group, phase):
        streams = RS_GROUPS[group]
        n = layer * 3 + group
        if phase == 0:
            cols = (streams[0][0], streams[2][1])
            src = held(dG.at[layer], dict(z=ALL, c=beside("c", 1)["c"], y=ALL, x=ALL), cols)
            dst = recvC.at[:, :, :, :, pl.ds(cols[0], cols[1] - cols[0])]
            return [remote(src, dst, rsc_s.at[n], rsc_r.at[n], beside("c", 1))]
        out = []
        for s, cols in enumerate(streams):
            order = RS_ORDERS[s]
            window = pl.ds(cols[0], cols[1] - cols[0])
            for d in (1, 2, 3):
                peer = beside(order[phase - 1], d)
                at = dict(z=ALL, c=me["c"], y=ALL, x=ALL)
                for axis in order[: phase - 1]:
                    at[axis] = me[axis]
                at[order[phase - 1]] = peer[order[phase - 1]]
                src = held(dG.at[layer], at, cols)
                if phase == 1:
                    dst = R1.at[d - 1, :, :, :, window]
                elif phase == 2:
                    dst = R2.at[layer, d - 1, :, :, window]
                else:
                    dst = R3.at[layer, d - 1, :, window]
                m = (phase - 1) * 3 + d - 1
                out.append(remote(src, dst, rs_s.at[n, s, m], rs_r.at[n, s, m], peer))
        return out

    def rs_sum(layer, group, phase):
        streams = RS_GROUPS[group]
        if phase == 0:
            first, last = streams[0][0], streams[2][1]

            def add(i, carry):
                z, y = lax.div(i, 4), lax.rem(i, 4)
                mine = dG[layer, z, me["c"], y, :, :, first:last].astype(F32)
                other = recvC[z, y, :, :, first:last].astype(F32)
                dG[layer, z, me["c"], y, :, :, first:last] = (mine + other).astype(BF16)
                return carry

            lax.fori_loop(0, 16, add, 0)
            return
        for s, (first, last) in enumerate(streams):
            order = RS_ORDERS[s]
            left = rest(order, phase)
            if phase == 1:

                def add(i, carry, left=left, order=order, first=first, last=last):
                    u = lax.div(i, 4)
                    v = lax.rem(i, 4)
                    at = {left[0]: u, left[1]: v, order[0]: me[order[0]]}
                    total = dG[layer, at["z"], me["c"], at["y"], at["x"], :, first:last].astype(F32)
                    for d in range(3):
                        total = total + R1[d, u, v, :, first:last].astype(F32)
                    dG[layer, at["z"], me["c"], at["y"], at["x"], :, first:last] = total.astype(BF16)
                    return carry

                lax.fori_loop(0, 16, add, 0)
            elif phase == 2:

                def add(u, carry, left=left, order=order, first=first, last=last):
                    at = dict(me)
                    at[left[0]] = u
                    total = dG[layer, at["z"], me["c"], at["y"], at["x"], :, first:last].astype(F32)
                    for d in range(3):
                        total = total + R2[layer, d, u, :, first:last].astype(F32)
                    dG[layer, at["z"], me["c"], at["y"], at["x"], :, first:last] = total.astype(BF16)
                    return carry

                lax.fori_loop(0, 4, add, 0)
            else:
                total = dG[layer, me["z"], me["c"], me["y"], me["x"], :, first:last].astype(F32)
                for d in range(3):
                    total = total + R3[layer, d, :, first:last].astype(F32)
                fin[layer, :, first:last] = total

    def rs_step(layer, group, phase):
        if phase > 0:
            copies = rs_copies(layer, group, phase - 1)
            arrive(copies)
            leave(copies)
            rs_sum(layer, group, phase - 1)
        if phase < 4:
            start(rs_copies(layer, group, phase))

    start(x_copies())
    vsum[...] = vec_ref[...]
    start(vec_copies("x", vsum, vrecv, v_s, v_r, 0))
    xin[me["x"]] = blocks_ref[me["x"]]
    for layer in range(LAYERS):
        G[layer, me["z"], me["c"], me["y"], me["x"], :, OUTER : OUTER + 512] = outer_ref[layer]
    H[0, 0] = x_ref[...].astype(F32)
    row = lax.broadcasted_iota(jnp.int32, (64, 64), 0)
    col = lax.broadcasted_iota(jnp.int32, (64, 64), 1)

    def swap_groups(v):
        return (v & 3) | ((v & 12) << 2) | ((v & 48) >> 2)

    perm = jnp.where(swap_groups(row) == col, 1.0, 0.0).astype(BF16)
    arrive(x_copies())
    mixed_rows = dot(perm, xin[...].reshape(64, 768)).astype(BF16)
    for layer in range(LAYERS):
        for kk in range(4):
            G[layer, me["z"], me["c"], me["y"], me["x"], :, kk * 384 : (kk + 1) * 384] = mixed_rows[
                kk * 16 : (kk + 1) * 16, layer * 384 : (layer + 1) * 384
            ]
    ag_step(0, 0)

    def vec_sum(buf, recv, copies, slot, count):
        arrive(copies)
        leave(copies)
        total = buf[...].astype(F32)
        for d in range(count):
            total = total + recv[slot, d].astype(F32)
        buf[...] = total.astype(buf.dtype)

    vec_sum(vsum, vrecv, vec_copies("x", vsum, vrecv, v_s, v_r, 0), 0, 3)
    start(vec_copies("y", vsum, vrecv, v_s, v_r, 1))
    ag_step(0, 1)
    ag_step(1, 0)
    vec_sum(vsum, vrecv, vec_copies("y", vsum, vrecv, v_s, v_r, 1), 1, 3)
    start(vec_copies("z", vsum, vrecv, v_s, v_r, 2))
    ag_step(0, 2)
    ag_step(1, 1)
    vec_sum(vsum, vrecv, vec_copies("z", vsum, vrecv, v_s, v_r, 2), 2, 3)
    start(vec_copies("c", vsum, vrecv, v_s, v_r, 3))
    vec_sum(vsum, vrecv, vec_copies("c", vsum, vrecv, v_s, v_r, 3), 3, 1)
    vecs = vsum[...].astype(F32)
    for j in range(LAYERS * VECS):
        VB[j] = jnp.concatenate([vecs[4 * j + t : 4 * j + t + 1, :] for t in range(4)], axis=1)
    ag_step(0, 3)
    ln_forward(0, 0)
    ag_step(0, 4)

    def fsrc(y, x):
        return PK.at[y, x]

    def osrc(y, x):
        return osend.at[y * 4 + x]

    def usrc(y, x):
        return upsend.at[y, x]

    def dsrc(y, x):
        return dsend.at[y * 4 + x]

    for layer in range(LAYERS):
        if layer > 0:
            ln_forward(layer, 0)
        project(layer, 0, PK)
        a2a_start(layer * 4, fsrc, QK.at[layer, fs])
        if layer == 0:
            ag_step(1, 2)
        a2a_wait(layer * 4, fsrc, QK.at[layer, fs])
        sample_forward(layer)
        a2a_start(layer * 4 + 1, osrc, MX.at[layer, me["y"], me["x"]])
        if layer == 0:
            ag_step(1, 3)
            ag_step(2, 0)
        a2a_wait(layer * 4 + 1, osrc, MX.at[layer, me["y"], me["x"]])
        if layer == 0:
            ag_step(1, 4)
            ag_step(2, 1)
        attention_out(layer, 0, MX.at[layer])
        ln_forward(layer, 1)
        project(layer, 1, PKF.at[layer])
        if layer == 0:
            ag_step(2, 2)
        feature_forward(layer)
        attention_out(layer, 1, MXF.at[layer])
        ff_forward(layer, layer == LAYERS - 1)
        if layer == 0:
            ag_step(2, 3)
            ag_step(2, 4)

    g_ref[...] = seed_ref[...].astype(F32)
    for layer in (1, 0):
        ff_backward(layer)
        if layer == 0:
            rs_step(1, 2, 1)
        rs_step(layer, 0, 0)
        if layer == 0:
            rs_step(1, 1, 3)
        attention_out_backward(layer, 1, MXF.at[layer])
        feature_backward(layer)
        rs_step(layer, 0, 1)
        if layer == 0:
            rs_step(1, 2, 2)
            rs_step(1, 1, 4)
        project_backward(layer, 1)
        rs_step(layer, 1, 0)
        attention_out_backward(layer, 0, MX.at[layer])
        a2a_start(layer * 4 + 2, usrc, uprecv.at[layer, fs])
        rs_step(layer, 0, 2)
        if layer == 0:
            rs_step(1, 2, 3)
        a2a_wait(layer * 4 + 2, usrc, uprecv.at[layer, fs])
        sample_backward(layer)
        a2a_start(layer * 4 + 3, dsrc, drecv.at[me["y"], me["x"]])
        rs_step(layer, 0, 3)
        rs_step(layer, 1, 1)
        if layer == 0:
            rs_step(1, 2, 4)
        a2a_wait(layer * 4 + 3, dsrc, drecv.at[me["y"], me["x"]])
        project_backward(layer, 0)
        rs_step(layer, 2, 0)
        rs_step(layer, 1, 2)
        rs_step(layer, 0, 4)
    gout_ref[...] = g_ref[...]

    gv = functools.partial(vec_copies, buf=gsum, recv=grecv, ss=gv_s, rs=gv_r)
    start(gv("x", slot=0))
    rs_step(0, 2, 1)
    vec_sum(gsum, grecv, gv("x", slot=0), 0, 3)
    start(gv("y", slot=1))
    rs_step(0, 1, 3)
    rs_step(0, 2, 2)
    vec_sum(gsum, grecv, gv("y", slot=1), 1, 3)
    start(gv("z", slot=2))
    rs_step(0, 1, 4)
    rs_step(0, 2, 3)
    vec_sum(gsum, grecv, gv("z", slot=2), 2, 3)
    start(gv("c", slot=3))
    rs_step(0, 2, 4)
    vec_sum(gsum, grecv, gv("c", slot=3), 3, 1)
    vecout_ref[...] = gsum[...]
    w2out_ref[...] = fin[:, :, OUTER : OUTER + 512]
    stacked = jnp.concatenate(
        [
            jnp.concatenate([fin[l, :, kk * 384 : (kk + 1) * 384] for l in range(LAYERS)], axis=1)
            for kk in range(4)
        ],
        axis=0,
    ).astype(BF16)
    xout[...] = dot(perm, stacked).astype(BF16).reshape(4, 16, 768)

    def xf_copies():
        return [
            remote(
                xout.at[beside("x", d)["x"]],
                xfin.at[me["x"]],
                xs_s.at[1, d - 1],
                xs_r.at[1, d - 1],
                beside("x", d),
            )
            for d in (1, 2, 3)
        ]

    start(xf_copies())
    xfin[me["x"]] = xout[me["x"]]
    arrive(xf_copies())
    wout_ref[...] = xfin[...].astype(F32)
    leave(xf_copies())
    leave(x_copies())
    for group in range(3):
        for phase in range(4):
            leave(ag_copies(group, phase))


def vmem(shape, dtype):
    return pltpu.VMEM(shape, dtype)


def layers(x, seed, blocks, outer, vec, kmask, fmask):
    dma = pltpu.SemaphoreType.DMA
    whole = pl.BlockSpec(memory_space=pltpu.VMEM)
    return pl.pallas_call(
        kernel,
        out_shape=(
            jax.ShapeDtypeStruct((TOK, DIM), F32),
            jax.ShapeDtypeStruct((TOK, DIM), F32),
            jax.ShapeDtypeStruct((4, 16, 768), F32),
            jax.ShapeDtypeStruct((LAYERS, 16, 512), F32),
            jax.ShapeDtypeStruct((80, 128), F32),
        ),
        in_specs=[whole] * 7,
        out_specs=(whole,) * 5,
        scratch_shapes=[
            vmem((2, 4, 2, 4, 4, 16, 2048), BF16),
            vmem((2, 4, 2, 4, 4, 16, 2048), BF16),
            vmem((4, 4, 4, 16, 2048), BF16),
            vmem((3, 4, 4, 16, 2048), BF16),
            vmem((2, 3, 4, 16, 2048), BF16),
            vmem((2, 3, 16, 2048), BF16),
            vmem((2, 16, 2048), F32),
            vmem((4, 16, 768), BF16),
            vmem((4, 16, 768), BF16),
            vmem((4, 16, 768), BF16),
            vmem((80, 128), BF16),
            vmem((4, 3, 80, 128), BF16),
            vmem((20, 1, 512), F32),
            vmem((80, 128), F32),
            vmem((4, 3, 80, 128), F32),
            vmem((2, 3, TOK, DIM), F32),
            vmem((4, 4, 64, 384), BF16),
            vmem((2, 16, 64, 384), BF16),
            vmem((2, 4, 4, 64, 384), BF16),
            vmem((2, 4, 4, 64, 128), BF16),
            vmem((2, 4, 4, 64, 128), BF16),
            vmem((2, 2, 4, 1, 256), F32),
            vmem((2, 2, 4, 1, 256), F32),
            vmem((16, 64, 128), BF16),
            vmem((4, 4, 64, 128), BF16),
            vmem((2, 16, 64, 128), BF16),
            vmem((16, 64, 384), BF16),
            vmem((4, 4, 64, 384), BF16),
            vmem((2, 1024, 128), BF16),
            vmem((2, 1024, 128), BF16),
            vmem((128, 1024), BF16),
            vmem((2, 1024, 128), F32),
            vmem((2, 1024, 128), F32),
            vmem((TOK, DIM), BF16),
            vmem((TOK, DIM), BF16),
            vmem((TOK, DIM), F32),
            vmem((TOK, DIM), F32),
            dma((8, 16)),
            dma((8, 16)),
            dma((3, 3, 9)),
            dma((3, 3, 9)),
            dma((3,)),
            dma((3,)),
            dma((6, 3, 9)),
            dma((6, 3, 9)),
            dma((6,)),
            dma((6,)),
            dma((2, 3)),
            dma((2, 3)),
            dma((4, 3)),
            dma((4, 3)),
            dma((4, 3)),
            dma((4, 3)),
        ],
        compiler_params=pltpu.CompilerParams(
            collective_id=0, has_side_effects=True, vmem_limit_bytes=63 * 2**20
        ),
    )(x, seed, blocks, outer, vec, kmask, fmask)


def body(
    entry_embeddings,
    norm_scales,
    triple_entry_matrix,
    mixing_exit_matrix,
    exit_bias,
    expanding_matrix,
    former_dense_bias,
    contracting_matrix,
    latter_dense_bias,
    row_presence_indicator,
    problem_column_number,
    loss_gradient,
):
    fs = lax.axis_index("fsdp")
    me = lax.axis_index("dp") * 16 + fs
    sample_ok = row_presence_indicator[0] > 0
    local_ok = lax.dynamic_slice_in_dim(sample_ok, fs * 64, 64)
    feature_ok = jnp.arange(4, dtype=jnp.int32) < problem_column_number[0]
    keep = feature_ok[:, None] & local_ok[None, :]

    x = entry_embeddings[0].transpose(1, 0, 2).reshape(TOK, DIM)
    seed = loss_gradient[0].transpose(1, 0, 2)
    seed = jnp.where(keep[:, :, None], seed, jnp.zeros_like(seed)).reshape(TOK, DIM)

    heads = triple_entry_matrix.reshape(2, 2, 4, 3, 4, 128)
    merge = mixing_exit_matrix.reshape(2, 2, 4, 1, 4, 128)
    chunks = jnp.concatenate([heads, merge], axis=3)
    chunks = chunks.transpose(4, 0, 2, 1, 3, 5).reshape(4, 2, 4, 8, 128)
    inner = expanding_matrix.reshape(2, 4, 4, 4, 128).transpose(2, 0, 1, 3, 4)
    chunks = jnp.concatenate([chunks, inner], axis=3).reshape(4, 2, 4, 4, 3, 128)
    blocks = chunks.transpose(0, 3, 2, 1, 4, 5).reshape(4, 16, 768)

    small = jnp.concatenate([norm_scales, exit_bias, latter_dense_bias[:, None]], axis=1)
    place = jnp.arange(512, dtype=jnp.int32) // 4 == me
    small = jnp.where(place, jnp.tile(small, (1, 1, 128)), 0).reshape(2, 24, 128)
    place = jnp.arange(2048, dtype=jnp.int32) // 16 == me
    large = jnp.where(place, jnp.tile(former_dense_bias, (1, 128)), 0).reshape(2, 16, 128)
    vec = jnp.concatenate([small, large], axis=1).reshape(80, 128).astype(BF16)

    kmask = jnp.where(sample_ok[:, None], 0.0, NEG).astype(BF16)
    kmask = jnp.broadcast_to(kmask, (1024, 128))
    key = jnp.arange(TOK, dtype=jnp.int32)
    same = (key[:, None] % 64 == key[None, :] % 64) & (key // 64 < problem_column_number[0])[:, None]
    fmask = jnp.where(same, 0.0, NEG).astype(F32)

    h, g, w, w2, vecs = layers(x, seed, blocks, contracting_matrix, vec, kmask, fmask)

    h = jnp.where(keep[:, :, None], h.reshape(4, 64, DIM), 0.0).transpose(1, 0, 2)
    g = g.reshape(4, 64, DIM).transpose(1, 0, 2)
    w = w.reshape(4, 4, 4, 2, 3, 128)
    w = w.transpose(3, 2, 1, 4, 0, 5).reshape(2, 4, 12, 4, 128)
    delta_heads = jnp.stack(
        [w[:, :, 0:3].reshape(2, 4, 1536), w[:, :, 4:7].reshape(2, 4, 1536)], axis=1
    )
    delta_merge = jnp.stack([w[:, :, 3].reshape(2, 4, 512), w[:, :, 7].reshape(2, 4, 512)], axis=1)
    delta_inner = w[:, :, 8:12].transpose(0, 1, 3, 2, 4).reshape(2, 4, 2048)
    vecs = vecs.reshape(2, 40 * 128)
    small = lax.dynamic_slice_in_dim(vecs[:, : 6 * 512].reshape(2, 6, 512), me * 4, 4, 2)
    thresholds = lax.dynamic_slice_in_dim(vecs[:, 6 * 512 :], me * 16, 16, 1)
    return (
        h[None],
        g[None],
        small[:, 0:3],
        delta_heads,
        delta_merge,
        small[:, 3:5],
        delta_inner,
        thresholds,
        w2,
        small[:, 5],
    )


def solution(mesh):
    both = ("dp", "fsdp")
    tokens = P("dp", "fsdp", None, None)
    weights = (
        P(None, None, both),
        P(None, None, both, None),
        P(None, None, both, None),
        P(None, None, both),
        P(None, both, None),
        P(None, both),
        P(None, both, None),
        P(None, both),
    )
    return jax.shard_map(
        body,
        mesh=mesh,
        in_specs=(tokens,) + weights + (P("dp", None), P("dp"), tokens),
        out_specs=(tokens, tokens) + weights,
        check_vma=False,
    )
```

time: 2590 us -> 293 us (0.11)
  waiting for transfers between devices: 1730 us -> 0 us
  blocking collectives: 401 us -> 0 us
  Pallas kernels: 0 us -> 268 us
  matrix products: 176 us -> 0 us
  local copies, waits for them, and re-layouts: 188 us -> 12.8 us
  other arithmetic: 63 us -> 7.12 us
    reduce_scatter x4 -> x0, waiting for transfers between devices: 1370 us -> none  [the longest x2 1250 us: body(): lax.psum_scatter(delta_outer, ('dp', 'fsdp'), scatter_dimension=0, tiled=...]
    pallas_call x0 -> x1, Pallas kernels: none -> 268 us  [layers(): pl.pallas_call(kernel, out_shape=(jax.ShapeDtypeStruct((TOK, DIM), F32),...]
    all_gather x4 -> x0, blocking collectives: 239 us -> none  [the longest x2 122 us: body(): lax.all_gather(norm_scales[apply_block], ('dp', 'fsdp'), axis=1, tiled=True)]
    all_gather x10 -> x0, waiting for transfers between devices: 198 us -> none  [the longest x2 112 us: body(): lax.all_gather(contracting_matrix[apply_block], ('dp', 'fsdp'), axis=0, t...]
    dot_general x60 -> x0, matrix products: 176 us -> none  [the longest x12 26.2 us: project_back(): jnp.einsum('sfe,de->sfd', left, right, preferred_element_type=jnp.float32)]
    unnamed x16 -> x0, waiting for transfers between devices: 164 us -> none
    unnamed x2 -> x0, blocking collectives: 161 us -> none
    slice x24 -> x7, local copies, waits for them, and re-layouts: 78.9 us -> 1.39 us  [the longest x1 0.65 us: body(): small[:, 3:5]]
  transfers between devices with their start and end apart: 15 -> 0, of which waited for: 9 -> 0; matrix products, arithmetic and copies ran while one was open for 9% -> 0% of each run, Pallas kernels for 0% -> 0%
where the time goes in v1:
time: 293 us; the launch traced here: 290 us
  Pallas kernels  268 us (91%)
  local copies, waits for them, and re-layouts  12.8 us (4%)
  other arithmetic  7.12 us (2%)
    pallas_call x1, Pallas kernels, layers(): pl.pallas_call(kernel, out_shape=(jax.ShapeDtypeStruct((TOK, DIM), F32),...  268 us

profile of v1, /device:TPU:1, one launch (start us, length us, event | category | flops | bytes accessed | tf_op | source)
XLA Modules:
  0.0 289.9 jit_solution(2828415414204560181)
XLA Ops:
  0.7 0.7 copy-done.7
  1.3 0.1 dynamic-slice_bitcast_fusion
  2.1 0.1 broadcast_and_fusion
  2.2 1.2 bitcast_select_fusion
  3.3 0.7 copy.50
  4.1 0.7 copy-done.9
  4.8 0.7 copy-done.8
  5.6 0.5 tile.9
  6.1 0.6 copy-done.10
  6.8 0.1 tile.21
  6.9 0.6 pad_maximum_fusion.4
  7.5 0.8 and_select_fusion.fmask_ref
  8.4 0.7 copy-done.6
  9.2 0.7 copy-done.5
  10.1 0.7 reshape.190.blocks_ref
  10.9 0.9 broadcast_in_dim.90.kmask_ref
  11.8 0.7 copy.49
  12.5 268.5 %shard_map.195 = (f32[256,512]{1,0:T(8,128)}, f32[256,512]{1,0:T(8,128)}, f32[4,16,768]{2,1,0:T(8,128)}, f32[2,16,512]{2,1,0:T(8,128)}, f32[80,128]{1,0:T(8,128)}) custom-call(bf16[256,512]{1,0:T(8,128)(2,1)} %bitcast.49, bf16[256,512]{1,0:T(8,128)(2,1)} %bitcast.48, bf16[4,16,768]{2,1,0:T(8,128)(2,1)} %reshape.190.blocks_ref, ...), custom_call_target="tpu_custom_call" | custom-call | tf_op jit(solution)/shard_map/pallas_call | solution.py:823
  281.0 2.9 %copy_bitcast_fusion = (f32[1,64,4,512]{3,2,1,0:T(4,128)}, f32[1,64,4,512]{3,2,1,0:T(4,128)}) fusion(f32[4,64,512]{2,1,0:T(8,128)} %bitcast.54, f32[4,64,512]{2,1,0:T(8,128)} %bitcast.53, pred[4,64]{0,1:T(8,128)(4,1)S(1)} %broadcast_and_fusion), kind=kLoop, calls=%fused_computation | loop fusion | flops 131072 | bytes 2097408 | tf_op jit(solution)/shard_map/broadcast_in_dim | solution.py:957
  284.0 0.1 reshape.196
  284.1 0.1 copy.60
  284.3 0.6 pad_maximum_fusion.3
  285.0 0.7 pad_maximum_fusion.1
  285.7 0.1 copy-done.4
  285.8 0.1 constant_dynamic-slice_fusion.1
  285.9 0.6 copy.66
  286.5 0.7 constant_dynamic-slice_fusion
  287.1 0.6 constant_dynamic-slice_fusion.3
  287.8 0.6 constant_dynamic-slice_fusion.2
  288.5 0.7 reshape.198
  289.1 0.2 copy-done.2
  289.3 0.6 copy.75
  (53 shorter events, 0.7 us)
Async XLA Ops:
  0.6 0.7 copy-start.7
  4.1 0.7 copy-start.9
  4.8 0.7 copy-start.8
  4.8 0.7 copy-start.11
  6.1 0.7 copy-start.10
  7.5 0.8 copy-start.3
  8.4 0.7 copy-start.6
  9.1 0.8 copy-start.5
  10.1 1.7 copy-start
  281.0 3.0 %copy-start.1 = (f32[4,16,768]{2,1,0:T(8,128)S(1)}, f32[4,16,768]{2,1,0:T(8,128)}, u32[]{:S(2)}) copy-start(f32[4,16,768]{2,1,0:T(8,128)} %get-tuple-element.18) | copy-start | bytes 589828
  285.0 0.8 copy-start.4
  288.4 0.8 copy-start.2
